TPU v7x, 32 devices: a whole 2x2x4 slice. The times are simulated.
32 devices in a mesh: ctx: 4 (over y, core), exp: 8 (over z, x).
Axes of the slice: x: 2, y: 2, z: 4, core: 2. Of those that a mesh axis runs over, the one named last changes fastest.
Arguments:
- prompt_cache: bfloat16 [12288, 576], P('ctx'), may hold values from -8 to 8
- tree_latent: bfloat16 [256, 576], P('ctx'), may hold values from -12 to 12
- parents: int32 [256], replicated, may hold values from -1 to 254, as said below
- query_nope: bfloat16 [256, 128, 128], P(None, 'exp'), may hold values from -8 to 8
- query_rope: bfloat16 [256, 128, 64], P(None, 'exp'), may hold values from -400 to 400
- w_absorb: bfloat16 [128, 128, 512], P('exp'), may hold values from -0.5 to 0.5
- w_value: bfloat16 [128, 512, 128], P('exp'), may hold values from -2 to 2
- w_out: bfloat16 [16384, 7168], P('exp', 'ctx'), may hold values from -0.046875 to 0.046875
- residual: bfloat16 [256, 7168], P('exp', 'ctx'), may hold values from -400 to 400
- norm_gain: bfloat16 [7168], P('ctx'), may hold values from 0.5 to 1.5
- routes: int32 [256, 8], replicated, may hold values from 0 to 31, all different within a row; in each aligned block of 32 rows (0 to 31, 32 to 63, ...) at most 16 rows name the same one
- route_weights: float32 [256, 8], replicated, may hold values from 0.1 to 1
- w_gate: bfloat16 [32, 7168, 1024], P('exp', 'ctx'), may hold values from -0.0625 to 0.0625
- w_up: bfloat16 [32, 7168, 1024], P('exp', 'ctx'), may hold values from -0.0625 to 0.0625
- w_down: bfloat16 [32, 1024, 7168], P('exp', None, 'ctx'), may hold values from -0.1875 to 0.1875
Outputs:
- attn_out: bfloat16 [256, 7168], P('exp', 'ctx')
- moe_out: bfloat16 [256, 7168], P('exp', 'ctx')
Inputs may be any that keep to these rules, and one draw needn't show every extreme that they name: `routes`: each row names 8 different experts. No expert is named by more than 16 rows of one aligned block of 32 rows, and that bound is reached. parents[0] = -1; every other node's parent is an earlier node, at most 24 positions before it; the last node's parent is the node just before it.
All inputs are finite; a program needn't handle non-finite values.
Results may differ from a plain program's by a relative error of at most 0.035.
Values may be sent and summed in bfloat16 or wider, within the bound.
A program may use at most 256 MiB of HBM per device.

v0:
```python
import jax
import jax.numpy as jnp
from jax import lax
from jax.sharding import PartitionSpec as P

D = 7168
TOPK = 8
EXPERTS = 32


NEG_FILL = -1e30
EXACT_PRODUCTS = lax.Precision.HIGHEST


def merged(array, axis, join):
    gathered = jax.tree.map(
        lambda a, kind: lax.all_gather(a.astype(kind), axis),
        array,
        (jnp.bfloat16, jnp.bfloat16, jnp.bfloat16),
    )

    def take(source):
        return jax.tree.map(
            lambda a, own: lax.dynamic_index_in_dim(a, source, 0, False).astype(own.dtype),
            gathered,
            array,
        )

    return lax.fori_loop(
        1, lax.axis_size(axis), lambda source, state: join(state, take(source)), take(0)
    )


def ancestry(parents):
    node_total = parents.shape[0]
    linked = (parents[:, None] == jnp.arange(node_total, dtype=jnp.int32)[None, :]).astype(
        jnp.float32
    )
    ancestors = jnp.eye(node_total, dtype=jnp.float32) + linked
    for repeat in range(node_total.bit_length()):
        ancestors = jnp.minimum(jnp.dot(ancestors, ancestors, precision=EXACT_PRODUCTS), 1.0)
    return ancestors


def slot_ranks(routes, block_rows):
    onehot = (routes[:, :, None] == jnp.arange(EXPERTS, dtype=jnp.int32)).astype(jnp.int32)
    grouped = onehot.reshape(-1, block_rows * TOPK, EXPERTS)
    before = jnp.cumsum(grouped, axis=1) - grouped
    return jnp.sum(before * grouped, axis=2).reshape(routes.shape)


def merge_parts(earlier, latter):
    first_top, first_total, first_mix = earlier
    second_top, second_total, second_mix = latter
    top_score = jnp.maximum(first_top, second_top)
    first_factor = jnp.exp(first_top - top_score)
    second_factor = jnp.exp(second_top - top_score)
    weight_total = first_total * first_factor + second_total * second_factor
    combined = first_mix * first_factor[..., None] + second_mix * second_factor[..., None]
    return (top_score, weight_total, combined)


def combine_parts(top_score, weight_total, partial_mix):
    return merged((top_score, weight_total, partial_mix), "ctx", merge_parts)


def expert_block(pieces, w_gate, w_up, w_down):
    blocks, squares = pieces
    gate_part = jnp.einsum("sjkd,jdf->sjkf", blocks, w_gate, preferred_element_type=jnp.float32)
    up_part = jnp.einsum("sjkd,jdf->sjkf", blocks, w_up, preferred_element_type=jnp.float32)
    gate_sum, up_sum, square_sum = (
        lax.psum(gate_part.astype(jnp.bfloat16), "ctx").astype(jnp.float32),
        lax.psum(up_part.astype(jnp.bfloat16), "ctx").astype(jnp.float32),
        lax.psum(squares.astype(jnp.float32).astype(jnp.bfloat16), "ctx").astype(jnp.float32),
    )
    root_mean = jnp.sqrt(square_sum / D + 1e-06)[..., None]
    expert_hidden = (jax.nn.silu(gate_sum / root_mean) * (up_sum / root_mean)).astype(jnp.bfloat16)
    return jnp.einsum(
        "sjkf,jfd->sjkd", expert_hidden, w_down, preferred_element_type=jnp.float32
    ).astype(jnp.bfloat16)


def body(
    prompt_cache,
    tree_latent,
    parents,
    query_nope,
    query_rope,
    w_absorb,
    w_value,
    w_out,
    residual,
    norm_gain,
    routes,
    route_weights,
    w_gate,
    w_up,
    w_down,
):
    node_total, heads_here, nope_width = query_nope.shape
    latent_width = w_absorb.shape[2]
    score_scale = (nope_width + query_rope.shape[2]) ** (-0.5)
    dims_last = (((1,), (1,)), ((), ()))
    absorbed = jnp.einsum(
        "nhc,hcl->nhl", query_nope, w_absorb, preferred_element_type=jnp.float32
    ).astype(jnp.bfloat16)
    queries = jnp.concatenate([absorbed, query_rope], axis=2).reshape(node_total * heads_here, -1)
    tree_rows = tree_latent.shape[0]
    ancestors = ancestry(parents)
    tree_columns = lax.dynamic_slice_in_dim(
        ancestors, lax.axis_index("ctx") * tree_rows, tree_rows, 1
    )
    prompt_scores = lax.dot_general(
        queries, prompt_cache, dims_last, preferred_element_type=jnp.float32
    )
    prompt_scores = prompt_scores.reshape(node_total, heads_here, -1) * score_scale
    tree_scores = lax.dot_general(
        queries, tree_latent, dims_last, preferred_element_type=jnp.float32
    )
    tree_scores = tree_scores.reshape(node_total, heads_here, -1) * score_scale
    tree_scores = jnp.where(tree_columns[:, None, :] > 0.5, tree_scores, NEG_FILL)
    top_score = jnp.maximum(jnp.max(prompt_scores, axis=2), jnp.max(tree_scores, axis=2))
    prompt_exp = jnp.exp(prompt_scores - top_score[..., None])
    tree_exp = jnp.exp(tree_scores - top_score[..., None])
    weight_total = jnp.sum(prompt_exp, axis=2) + jnp.sum(tree_exp, axis=2)
    latent_mix = jnp.dot(
        prompt_exp.reshape(node_total * heads_here, -1).astype(jnp.bfloat16),
        prompt_cache[:, :latent_width],
        preferred_element_type=jnp.float32,
    )
    latent_mix = latent_mix + jnp.dot(
        tree_exp.reshape(node_total * heads_here, -1).astype(jnp.bfloat16),
        tree_latent[:, :latent_width],
        preferred_element_type=jnp.float32,
    )
    latent_mix = latent_mix.reshape(node_total, heads_here, latent_width)
    value_weights = w_value.astype(jnp.float32)
    projected = jnp.einsum("nhl,hlv->nhv", latent_mix, value_weights, precision=EXACT_PRODUCTS)
    top_score, weight_total, projected = combine_parts(top_score, weight_total, projected)
    heads_out = (projected / weight_total[..., None]).astype(jnp.bfloat16).reshape(node_total, -1)
    row_count = residual.shape[0]
    attn_sum = lax.psum_scatter(
        jnp.dot(heads_out, w_out, preferred_element_type=jnp.float32).astype(jnp.bfloat16),
        "exp",
        scatter_dimension=0,
        tiled=True,
    ).astype(jnp.float32)
    state = residual.astype(jnp.float32) + attn_sum
    routed = (state * norm_gain.astype(jnp.float32)).astype(jnp.bfloat16)
    group_squares = jnp.sum(state * state, axis=1).astype(jnp.bfloat16)
    capacity = max(2, 2 * row_count * TOPK // EXPERTS)
    senders = lax.axis_size("exp")
    experts_here = w_gate.shape[0]
    exp_place = lax.axis_index("exp")
    own_routes = lax.dynamic_slice_in_dim(routes, exp_place * row_count, row_count, 0)
    own_weights = lax.dynamic_slice_in_dim(route_weights, exp_place * row_count, row_count, 0)
    slot_rank = slot_ranks(own_routes, row_count)
    expert_hot = (own_routes[:, :, None] == jnp.arange(EXPERTS, dtype=jnp.int32)).astype(
        jnp.float32
    )
    slot_hot = (slot_rank[:, :, None] == jnp.arange(capacity, dtype=jnp.int32)).astype(jnp.float32)
    placing = jnp.einsum("rkx,rks->xsr", expert_hot, slot_hot)
    send_blocks = jnp.einsum(
        "xsr,rd->xsd", placing.astype(jnp.bfloat16), routed, preferred_element_type=jnp.float32
    )
    send_blocks = send_blocks.astype(jnp.bfloat16).reshape(senders, experts_here, capacity, -1)
    send_squares = jnp.einsum(
        "xsr,r->xs", placing, group_squares.astype(jnp.float32), precision=EXACT_PRODUCTS
    )
    send_squares = send_squares.astype(jnp.bfloat16).reshape(senders, experts_here, capacity)
    answers = expert_block(
        (
            lax.all_to_all(send_blocks, "exp", split_axis=0, concat_axis=0, tiled=True),
            lax.all_to_all(send_squares, "exp", split_axis=0, concat_axis=0, tiled=True),
        ),
        w_gate,
        w_up,
        w_down,
    )
    returned = lax.all_to_all(answers, "exp", split_axis=0, concat_axis=0, tiled=True)
    returned = returned.reshape(EXPERTS, capacity, -1).astype(jnp.float32)
    weighting = jnp.einsum(
        "rkx,rks,rk->rxs", expert_hot, slot_hot, own_weights, precision=EXACT_PRODUCTS
    )
    moe_sum = jnp.einsum("rxs,xsd->rd", weighting, returned, precision=EXACT_PRODUCTS)
    return (attn_sum.astype(jnp.bfloat16), moe_sum.astype(jnp.bfloat16))


def solution(mesh):
    placed = (
        P("ctx", None),
        P("ctx", None),
        P(),
        P(None, "exp", None),
        P(None, "exp", None),
        P("exp", None, None),
        P("exp", None, None),
        P("exp", "ctx"),
        P("exp", "ctx"),
        P("ctx"),
        P(),
        P(),
        P("exp", "ctx", None),
        P("exp", "ctx", None),
        P("exp", None, "ctx"),
    )
    return jax.shard_map(
        body,
        mesh=mesh,
        in_specs=placed,
        out_specs=(P("exp", "ctx"), P("exp", "ctx")),
        check_vma=False,
    )
```

profile of v0, /device:TPU:0, one launch (start us, length us, event | category | flops | bytes accessed | tf_op | source)
XLA Modules:
  0.0 446.7 jit_solution(9086186341632601449)
XLA Ops:
  7.2 1.5 convolution_minimum_fusion.7
  8.7 0.4 convolution_minimum_fusion.6
  9.1 0.4 convolution_minimum_fusion.5
  9.5 0.4 convolution_minimum_fusion.4
  10.0 0.4 convolution_minimum_fusion.3
  10.4 0.4 convolution_minimum_fusion.2
  10.8 0.4 convolution_minimum_fusion.1
  11.2 0.4 convolution_minimum_fusion
  11.6 0.4 fusion.90
  12.0 3.3 convert_bitcast_fusion
  15.4 29.4 %multiply_reduce_fusion = (f32[256,16]{0,1:T(8,128)S(1)}, f32[256,16,3072]{2,0,1:T(8,128)}) fusion(bf16[3072,576]{0,1:T(8,128)(2,1)} %param.17, bf16[256,16,64]{0,2,1:T(8,128)(2,1)} %param.21, bf16[256,16,512]{0,2,1:T(8,128)(2,1)} %convert_bitcast_fusion), kind=kOutput, calls=%fused_computation.11 | convolution fusion | flops 14530113536 | bytes 58605568 | tf_op jit(solution)/shard_map/dot_general | solution.py:113
  44.8 2.8 fusion.89
  47.7 25.7 %fusion.3 = (bf16[256,16,3072]{2,0,1:T(8,128)(2,1)}, f32[256,16]{0,1:T(8,128)S(1)}) fusion(f32[256,16,3072]{2,0,1:T(8,128)} %get-tuple-element.243, f32[256,16]{0,1:T(8,128)S(1)} %get-tuple-element.237), kind=kLoop, calls=%fused_computation.12 | loop fusion | flops 50327552 | bytes 75530240 | tf_op jit(solution)/shard_map/convert_element_type | solution.py:127
  73.4 0.2 fusion.59
  73.6 1.0 copy.124
  74.5 4.4 fusion.80
  79.0 27.1 %copy.123 = bf16[256,16,3072]{2,1,0:T(8,128)(2,1)} copy(bf16[256,16,3072]{2,0,1:T(8,128)(2,1)} %get-tuple-element.238) | data formatting | bytes 50331648 | tf_op jit(solution)/shard_map/convert_element_type | solution.py:127
  106.1 22.4 %convolution_add_fusion = f32[4096,512]{1,0:T(8,128)} fusion(f32[4096,512]{1,0:T(8,128)} %fusion.80, bf16[4096,3072]{1,0:T(8,128)(2,1)} %bitcast.136, bf16[3072,576]{0,1:T(8,128)(2,1)} %param.17), kind=kOutput, calls=%fused_computation.22 | convolution fusion | flops 12886999040 | bytes 45088768 | tf_op jit(solution)/shard_map/dot_general | solution.py:126
  128.5 12.8 %fusion.39 = bf16[256,16,128]{2,0,1:T(8,128)(2,1)} fusion(bf16[16,512,128]{2,1,0:T(8,128)(2,1)S(1)} %copy-done.2, f32[256,16,512]{2,1,0:T(8,128)} %bitcast.138), kind=kOutput, calls=%fused_computation.42 | convolution fusion | flops 3221749760 | bytes 11534336 | tf_op jit(solution)/shard_map/nhl,hlv->nhv/dot_general | solution.py:138
  141.4 6.6 %all-gather = bf16[1024,16]{0,1:T(8,128)(2,1)S(1)} all-gather(bf16[256,16]{0,1:T(8,128)(2,1)S(1)} %get-tuple-element.236), channel_id=2, replica_groups=mesh['ctx'=4,'exp'=8] {'ctx'}, dimensions={0}, use_global_device_ids=true | all-gather | bytes 40960 | tf_op jit(solution)/shard_map/all_gather | solution.py:17
  148.1 5.4 %all-gather.1 = bf16[1024,16]{0,1:T(8,128)(2,1)S(1)} all-gather(bf16[256,16]{0,1:T(8,128)(2,1)S(1)} %add_convert_fusion), channel_id=3, replica_groups=mesh['ctx'=4,'exp'=8] {'ctx'}, dimensions={0}, use_global_device_ids=true | all-gather | bytes 40960 | tf_op jit(solution)/shard_map/all_gather | solution.py:17
  153.5 25.2 %all-gather.5.cloned.1.call-done = bf16[1024,16,128]{2,0,1:T(8,128)(2,1)} async-done(((bf16[256,16,128]{2,0,1:T(8,128)(2,1)}), bf16[1024,16,128]{2,0,1:T(8,128)(2,1)}) %all-gather.5.cloned.1.call-update) | async-done | bytes 4194320 | tf_op jit(solution)/shard_map/all_gather | solution.py:17
  178.7 1.4 slice_convert_fusion
  180.1 1.2 copy.126
  181.4 13.9 %while.19 = (s32[]{:T(128)}, f32[256,16]{0,1:T(8,128)S(1)}, f32[256,16]{0,1:T(8,128)S(1)}, f32[256,16,128]{2,1,0:T(8,128)S(1)}, bf16[4,256,16]{1,2,0:T(8,128)(2,...) while((s32[]{:T(128)}, f32[256,16]{0,1:T(8,128)S(1)}, ...), condition=%wide.region_5.6_spmd, body=%wide.region_4.5_spmd.sunk | while | flops 2129925 | bytes 7553175 | solution.py:29
  181.4 1.3 constant_dynamic-slice_fusion.4
  182.7 0.1 copy.199
  182.8 0.1 copy.200
  182.9 3.1 fusion.118
  186.0 1.3 constant_dynamic-slice_fusion.4
  187.4 0.1 copy.199
  187.5 0.1 copy.200
  187.6 3.1 fusion.118
  190.7 1.3 constant_dynamic-slice_fusion.4
  192.0 0.1 copy.199
  192.1 0.1 copy.200
  192.2 3.1 fusion.118
  195.3 0.1 copy.130
  195.4 0.7 divide_convert_fusion
  196.2 6.1 %convolution_convert_fusion.1 = bf16[256,1792]{1,0:T(8,128)(2,1)} fusion(bf16[2048,1792]{1,0:T(8,128)(2,1)} %param.24, bf16[32,8,16,128]{3,2,1,0:T(8,128)(2,1)S(1)} %bitcast.141), kind=kOutput, calls=%fused_computation.32 | convolution fusion | flops 1879506944 | bytes 9306112 | tf_op jit(solution)/shard_map/dot_general | solution.py:143
  202.5 0.1 eq.76
  202.6 0.6 reduce-window.6
  203.3 0.2 slice_reduce_fusion
  203.5 0.1 copy.135
  203.6 0.1 broadcast.54
  203.9 0.4 bitcast_convert_fusion
  204.3 0.2 copy.137
  204.5 61.2 %reduce-scatter.2.cloned.1.call-done = bf16[32,1792]{1,0:T(8,128)(2,1)} async-done(((bf16[256,1792]{1,0:T(8,128)(2,1)}), bf16[32,1792]{1,0:T(8,128)(2,1)}) %reduce-scatter.2.cloned.1.call-update) | async-done | bytes 114704 | tf_op jit(solution)/shard_map/reduce_scatter | solution.py:142
  265.7 1.5 convolution_convert_fusion
  267.2 44.2 %all_to_all.15 = bf16[8,4,16,1792]{3,2,1,0:T(8,128)(2,1)S(1)} all-to-all(bf16[8,4,16,1792]{3,2,1,0:T(8,128)(2,1)S(1)} %bitcast.139), channel_id=1, replica_groups=mesh['ctx'=4,'exp'=8] {'exp'}, dimensions={0} | all-to-all | bytes 3670016 | tf_op jit(solution)/shard_map/all_to_all | solution.py:173
  311.5 8.2 %fusion.42 = bf16[8,4,16,1024]{3,2,0,1:T(8,128)(2,1)} fusion(bf16[4,1792,1024]{2,1,0:T(8,128)(2,1)} %param.30, bf16[8,4,16,1792]{3,2,1,0:T(8,128)(2,1)S(1)} %all_to_all.15), kind=kOutput, calls=%fused_computation.43 | convolution fusion | flops 1879572480 | bytes 17563648 | tf_op jit(solution)/shard_map/sjkd,jdf->sjkf/dot_general | solution.py:70
  319.7 8.3 %fusion.47 = bf16[8,4,16,1024]{3,2,0,1:T(8,128)(2,1)} fusion(bf16[4,1792,1024]{2,1,0:T(8,128)(2,1)} %param.29, bf16[8,4,16,1792]{3,2,1,0:T(8,128)(2,1)S(1)} %all_to_all.15), kind=kOutput, calls=%fused_computation.44 | convolution fusion | flops 1879572480 | bytes 17563648 | tf_op jit(solution)/shard_map/sjkd,jdf->sjkf/dot_general | solution.py:69
  328.0 0.2 multiply_reduce_fusion.1
  328.2 0.1 fusion.61
  328.4 9.9 %all_to_all.16 = bf16[8,4,16]{2,1,0:T(4,128)(2,1)S(1)} all-to-all(bf16[8,4,16]{2,1,0:T(4,128)(2,1)S(1)} %bitcast.149), channel_id=1, replica_groups=mesh['ctx'=4,'exp'=8] {'exp'}, dimensions={0} | all-to-all | bytes 2048 | tf_op jit(solution)/shard_map/all_to_all | solution.py:174
  338.3 7.0 %psum.22 = bf16[8,4,16]{2,0,1:T(8,128)(2,1)S(1)} all-reduce(bf16[8,4,16]{2,0,1:T(8,128)(2,1)S(1)} %copy.139), channel_id=1, replica_groups=mesh['ctx'=4,'exp'=8] {'ctx'}, use_global_device_ids=true, to_apply=%region_12.13 | all-reduce | flops 512 | bytes 2048 | tf_op jit(solution)/shard_map/psum | solution.py:74
  345.3 33.7 %all-reduce.3.cloned.1.call-done = (bf16[8,4,16,1024]{3,2,0,1:T(8,128)(2,1)}, bf16[8,4,16,1024]{3,2,0,1:T(8,128)(2,1)}) async-done(((bf16[8,4,16,1024]{3,2,0,1:T(8,128)(2,1)}, bf16[8,4,16,1024]{3,2,0,1:T(8,128)(2,1)}), (bf16[8,4,16,1024]{3,2,0,1:T(8,128)(2,1)}, bf16[8,4,16,1024]{3,2,0,1:T(8,128)(2,1)})) %all-reduce.3.cloned.1.call-update) | async-done | bytes 2097168 | tf_op jit(solution)/shard_map/psum | solution.py:73
  379.0 8.2 %fusion.20 = bf16[8,4,16,1792]{3,2,0,1:T(8,128)(2,1)S(1)} fusion(bf16[4,1024,1792]{2,1,0:T(8,128)(2,1)} %param.31, bf16[8,4,16,1024]{3,2,0,1:T(8,128)(2,1)} %get-tuple-element.230, bf16[8,4,16,1024]{3,2,0,1:T(8,128)(2,1)} %get-tuple-element.231, f32[8,4,16]{2,0,1:T(8,128)S(1)} %add_sqrt_fusion), kind=kOutput, calls=%fused_computation.31 | convolution fusion | flops 1885208576 | bytes 18614272 | tf_op jit(solution)/shard_map/sjkf,jfd->sjkd/dot_general | solution.py:78
  387.2 1.4 copy.141
  388.6 5.5 %all-to-all-start.2 = ((bf16[8,4,16,1792]{3,2,1,0:T(8,128)(2,1)}), bf16[8,4,16,1792]{3,2,1,0:T(8,128)(2,1)}, u32[]{:S(2)}, u32[]{:S(2)}) async-start(bf16[8,4,16,1792]{3,2,1,0:T(8,128)(2,1)} %copy.141), calls=%async_computation.3 | async-start | bytes 3670016 | tf_op jit(solution)/shard_map/all_to_all | solution.py:180
  394.3 0.6 fusion.65
  394.9 0.2 copy.142
  395.1 41.7 %all-to-all-done.2 = bf16[8,4,16,1792]{3,2,1,0:T(8,128)(2,1)} async-done(((bf16[8,4,16,1792]{3,2,1,0:T(8,128)(2,1)}), bf16[8,4,16,1792]{3,2,1,0:T(8,128)(2,1)}, u32[]{:S(2)}, u32[]{:S(2)}) %all-to-all-start.2) | async-done | bytes 1835040 | tf_op jit(solution)/shard_map/all_to_all | solution.py:180
  436.8 3.2 fusion.23
  (54 shorter events, 1.1 us)
Async XLA Ops:
  7.2 4.9 %copy-start = (bf16[16,128,512]{2,1,0:T(8,128)(2,1)S(1)}, bf16[16,128,512]{2,1,0:T(8,128)(2,1)}, u32[]{:S(2)}) copy-start(bf16[16,128,512]{2,1,0:T(8,128)(2,1)} %param.22) | copy-start | bytes 6291460
  7.2 4.9 %copy-start.3 = (bf16[256,16,128]{2,1,0:T(8,128)(2,1)S(1)}, bf16[256,16,128]{2,1,0:T(8,128)(2,1)}, u32[]{:S(2)}) copy-start(bf16[256,16,128]{2,1,0:T(8,128)(2,1)} %param.20) | copy-start | bytes 3145732
  7.2 171.5 %all-gather.5.cloned.1.call-start = ((), (), s32[]{:S(2)}) async-start(), calls=%async_computation.5 | async-start | bytes 5242880 | tf_op jit(solution)/shard_map/all_gather | solution.py:17
  15.4 29.4 %copy-start.6 = (bf16[64,576]{1,0:T(8,128)(2,1)S(1)}, bf16[64,576]{1,0:T(8,128)(2,1)}, u32[]{:S(2)}) copy-start(bf16[64,576]{1,0:T(8,128)(2,1)} %param.18) | copy-start | bytes 221188
  15.4 29.4 %copy-start.10 = (bf16[256,16,64]{0,2,1:T(8,128)(2,1)S(1)}, bf16[256,16,64]{0,2,1:T(8,128)(2,1)}, u32[]{:S(2)}) copy-start(bf16[256,16,64]{0,2,1:T(8,128)(2,1)} %param.21) | copy-start | bytes 1572868
  106.1 22.4 %copy-start.2 = (bf16[16,512,128]{2,1,0:T(8,128)(2,1)S(1)}, bf16[16,512,128]{2,1,0:T(8,128)(2,1)}, u32[]{:S(2)}) copy-start(bf16[16,512,128]{2,1,0:T(8,128)(2,1)} %param.23) | copy-start | bytes 6291460
  141.4 124.3 %reduce-scatter.2.cloned.1.call-start = ((), (), s32[]{:S(2)}) async-start(), calls=%async_computation.4 | async-start | bytes 1032192 | tf_op jit(solution)/shard_map/reduce_scatter | solution.py:142
  196.1 6.2 %copy-start.8 = (s32[256,8]{0,1:T(8,128)S(1)}, s32[256,8]{0,1:T(8,128)}, u32[]{:S(2)}) copy-start(s32[256,8]{0,1:T(8,128)} %param.27) | copy-start | bytes 24580
  196.1 8.3 %copy-start.7 = (bf16[1792]{0:T(1024)(128)(2,1)S(1)}, bf16[1792]{0:T(1024)(128)(2,1)}, u32[]{:S(2)}) copy-start(bf16[1792]{0:T(1024)(128)(2,1)} %param.26) | copy-start | bytes 10756
  196.1 69.6 %copy-start.4 = (bf16[32,1792]{1,0:T(8,128)(2,1)S(1)}, bf16[32,1792]{1,0:T(8,128)(2,1)}, u32[]{:S(2)}) copy-start(bf16[32,1792]{1,0:T(8,128)(2,1)} %param.25) | copy-start | bytes 344068
  202.3 176.7 %all-reduce.3.cloned.1.call-start = ((), (), s32[]{:S(2)}) async-start(), calls=%async_computation.6 | async-start | bytes 4194304 | tf_op jit(solution)/shard_map/psum | solution.py:73
  319.7 8.3 %copy-start.5 = (bf16[32,1792]{1,0:T(8,128)(2,1)S(1)}, bf16[32,1792]{1,0:T(8,128)(2,1)}, u32[]{:S(2)}) copy-start(bf16[32,1792]{1,0:T(8,128)(2,1)} %reduce-scatter.2.cloned.1.call-done) | copy-start | bytes 344068
  387.2 6.9 %copy-start.9 = (f32[256,8]{0,1:T(8,128)S(1)}, f32[256,8]{0,1:T(8,128)}, u32[]{:S(2)}) copy-start(f32[256,8]{0,1:T(8,128)} %param.28) | copy-start | bytes 24580
  387.2 52.8 %copy-start.1 = (bf16[16,128,512]{2,1,0:T(8,128)(2,1)S(1)}, bf16[16,128,512]{2,1,0:T(8,128)(2,1)}, u32[]{:S(2)}) copy-start(bf16[16,128,512]{2,1,0:T(8,128)(2,1)} %param.22) | copy-start | bytes 6291460
  388.6 48.2 %all-to-all-start.2 = ((bf16[8,4,16,1792]{3,2,1,0:T(8,128)(2,1)}), bf16[8,4,16,1792]{3,2,1,0:T(8,128)(2,1)}, u32[]{:S(2)}, u32[]{:S(2)}) async-start(bf16[8,4,16,1792]{3,2,1,0:T(8,128)(2,1)} %copy.141), calls=%async_computation.3 | async-start | bytes 3670016 | tf_op jit(solution)/shard_map/all_to_all | solution.py:180
Sparse Core Ops, SparseCore 0:
  141.5 37.1 all-gather.4
  202.4 63.2 reduce-scatter.1
  328.1 50.8 all-reduce.2
where the time goes:
time: 452 us; the launch traced here: 447 us
  waiting for transfers between devices  162 us (36%)
  matrix products  116 us (26%)
  blocking collectives  73.2 us (16%)
  other arithmetic  38.4 us (8%)
  local copies, waits for them, and re-layouts  36.8 us (8%)
  between operations  14.3 us (3%)
  starting transfers between devices  5.63 us (1%)
    reduce_scatter x1, waiting for transfers between devices, body(): lax.psum_scatter(jnp.dot(heads_out, w_out, preferred_element_type=jnp.flo...  61.2 us
    all_to_all x1, blocking collectives, body(): lax.all_to_all(send_blocks, 'exp', split_axis=0, concat_axis=0, tiled=True)  44.2 us
    all_to_all x1, waiting for transfers between devices, body(): lax.all_to_all(answers, 'exp', split_axis=0, concat_axis=0, tiled=True)  41.7 us
    psum x1, waiting for transfers between devices, expert_block(): lax.psum(up_part.astype(jnp.bfloat16), 'ctx').astype(jnp.float32)  33.7 us
    dot_general x1, matrix products, body(): lax.dot_general(queries, prompt_cache, dims_last, preferred_element_type=...  29.4 us
    convert_element_type x1, local copies, waits for them, and re-layouts, body(): prompt_exp.reshape(node_total * heads_here, -1).astype(jnp.bfloat16)  27.1 us
    convert_element_type x1, other arithmetic, body(): prompt_exp.reshape(node_total * heads_here, -1).astype(jnp.bfloat16)  25.7 us
    all_gather x1, waiting for transfers between devices, merged(): lax.all_gather(a.astype(kind), axis)  25.2 us
  transfers between devices with their start and end apart: 4, of which 4 were waited for; matrix products, arithmetic and copies ran while one was open for 1% of the time, Pallas kernels for 0%

commit v1 on v0

--- a/solution.py
+++ b/solution.py
@@ -1,6 +1,8 @@
 import jax
 import jax.numpy as jnp
 from jax import lax
+from jax.experimental import pallas as pl
+from jax.experimental.pallas import tpu as pltpu
 from jax.sharding import PartitionSpec as P
 
 D = 7168
@@ -80,7 +82,7 @@
     ).astype(jnp.bfloat16)
 
 
-def body(
+def plain_body(
     prompt_cache,
     tree_latent,
     parents,
@@ -186,7 +188,616 @@
     return (attn_sum.astype(jnp.bfloat16), moe_sum.astype(jnp.bfloat16))
 
 
+LOG2E = 1.4426950408889634
+MESH = pl.DeviceIdType.MESH
+MIB = 1024 * 1024
+F32 = jnp.float32
+BF16 = jnp.bfloat16
+HEADS_PER_STEP = 2
+
+
+def attention_kernel(
+    scale, qn_ref, qr_ref, wabs_ref, wval_ref, cache_ref, tree_ref, linked_ref, select_ref,
+    part_ref, stat_ref, visible,
+):
+    step = pl.program_id(0)
+    nodes = qn_ref.shape[0]
+    latent = wabs_ref.shape[2]
+    nope = wabs_ref.shape[1]
+    vdim = wval_ref.shape[2]
+    heads = pl.num_programs(0) * HEADS_PER_STEP
+
+    @pl.when(step == 0)
+    def _():
+        reach = linked_ref[...]
+        for _ in range((nodes - 1).bit_length()):
+            reach = jnp.minimum(jnp.dot(reach, reach, preferred_element_type=F32), 1.0).astype(BF16)
+        visible[...] = jnp.dot(reach, select_ref[...], preferred_element_type=F32)
+        stat_ref[...] = jnp.zeros_like(stat_ref)
+
+    nt = (((1,), (1,)), ((), ()))
+    factor = scale * LOG2E
+    queries = jnp.concatenate(
+        [
+            jnp.concatenate(
+                [
+                    jnp.dot(
+                        qn_ref[:, h * nope : (h + 1) * nope], wabs_ref[h],
+                        preferred_element_type=F32,
+                    ).astype(BF16),
+                    qr_ref[h],
+                ],
+                axis=1,
+            )
+            for h in range(HEADS_PER_STEP)
+        ],
+        axis=0,
+    )
+    keys = cache_ref.shape[0]
+    chunk = 512
+    scores = [
+        lax.dot_general(
+            queries, cache_ref[at : at + chunk, :], nt, preferred_element_type=F32
+        ) * factor
+        for at in range(0, keys, chunk)
+    ]
+    tree_scores = lax.dot_general(queries, tree_ref[...], nt, preferred_element_type=F32) * factor
+    seen = jnp.concatenate([visible[...]] * HEADS_PER_STEP, axis=0)
+    tree_scores = jnp.where(seen > 0.5, tree_scores, NEG_FILL)
+    highest = scores[0]
+    for piece in scores[1:]:
+        highest = jnp.maximum(highest, piece)
+    top = jnp.maximum(
+        jnp.max(highest, axis=1, keepdims=True), jnp.max(tree_scores, axis=1, keepdims=True)
+    )
+    tree_exp = jnp.exp2(tree_scores - top)
+    total = jnp.sum(tree_exp, axis=1, keepdims=True)
+    mix = jnp.dot(tree_exp.astype(BF16), tree_ref[:, :latent], preferred_element_type=F32)
+    sums = None
+    for i, piece in enumerate(scores):
+        weight = jnp.exp2(piece - top)
+        sums = weight if sums is None else sums + weight
+        mix += jnp.dot(
+            weight.astype(BF16), cache_ref[i * chunk : (i + 1) * chunk, :latent],
+            preferred_element_type=F32,
+        )
+    total += jnp.sum(sums, axis=1, keepdims=True)
+    lane = lax.broadcasted_iota(jnp.int32, stat_ref.shape, 1)
+    stat = stat_ref[...]
+    for h in range(HEADS_PER_STEP):
+        rows = slice(h * nodes, (h + 1) * nodes)
+        head = step * HEADS_PER_STEP + h
+        part_ref[:, h * vdim : (h + 1) * vdim] = jnp.dot(
+            mix[rows].astype(BF16), wval_ref[h], preferred_element_type=F32
+        ).astype(BF16)
+        stat = jnp.where(lane == head, top[rows], stat)
+        stat = jnp.where(lane == heads + head, total[rows], stat)
+    stat_ref[...] = stat
+
+
+def attention(qn, qr, wabs, wval, cache, tree, linked, select):
+    nodes = qn.shape[0]
+    heads, nope, latent = wabs.shape
+    vdim = wval.shape[2]
+    rope = qr.shape[2]
+    per = HEADS_PER_STEP
+    whole = lambda a: pl.BlockSpec(a.shape, lambda i: (0,) * a.ndim)
+    scale = float((nope + rope) ** (-0.5))
+
+    def kernel(*refs):
+        attention_kernel(scale, *refs)
+
+    return pl.pallas_call(
+        kernel,
+        grid=(heads // per,),
+        out_shape=(
+            jax.ShapeDtypeStruct((nodes, heads * vdim), BF16),
+            jax.ShapeDtypeStruct((nodes, 128), F32),
+        ),
+        in_specs=[
+            pl.BlockSpec((nodes, per * nope), lambda i: (0, i)),
+            pl.BlockSpec((per, nodes, rope), lambda i: (i, 0, 0)),
+            pl.BlockSpec((per, nope, latent), lambda i: (i, 0, 0)),
+            pl.BlockSpec((per, latent, vdim), lambda i: (i, 0, 0)),
+            whole(cache), whole(tree), whole(linked), whole(select),
+        ],
+        out_specs=(
+            pl.BlockSpec((nodes, per * vdim), lambda i: (0, i)),
+            pl.BlockSpec((nodes, 128), lambda i: (0, 0)),
+        ),
+        scratch_shapes=[pltpu.VMEM((nodes, tree.shape[0]), F32)],
+        compiler_params=pltpu.CompilerParams(
+            dimension_semantics=("arbitrary",), vmem_limit_bytes=48 * MIB
+        ),
+        name="attention",
+    )(qn, qr, wabs, wval, cache, tree, linked, select)
+
+
+def places():
+    c = lax.axis_index("ctx")
+    e = lax.axis_index("exp")
+    core, z, x = c % 2, e // 2, e % 2
+    return c, e, core, z, x, c + 1 - 2 * core, c + 2 - 4 * (c // 2), e + 1 - 2 * x
+
+
+def greet():
+    c, e, core, z, x, sibling, across, xpeer = places()
+    barrier = pltpu.get_barrier_semaphore()
+    peers = [(sibling, e), (across, e), (c, xpeer)]
+    peers += [(c, (z + k) % 4 * 2 + x) for k in (1, 2, 3)]
+    for peer in peers:
+        pl.semaphore_signal(barrier, inc=1, device_id=peer, device_id_type=MESH)
+    pl.semaphore_wait(barrier, len(peers))
+
+
+def remote(src, dst, send, recv, to):
+    return pltpu.make_async_remote_copy(
+        src_ref=src, dst_ref=dst, send_sem=send, recv_sem=recv, device_id=to, device_id_type=MESH
+    )
+
+
+def block_of(index, rows):
+    return pl.ds(pl.multiple_of(index * rows, rows), rows)
+
+
+def scatter_sums(part, xbuf, zsend, zbuf, xs, xr, zs, zr, spans):
+    c, e, core, z, x, sibling, across, xpeer = places()
+    rows = zsend.shape[1]
+
+    def xcopy(j, k):
+        at, zt = spans[j], (z + k) % 4
+        return remote(
+            part.at[block_of(zt * 2 + 1 - x, rows), at], xbuf.at[k, :, at],
+            xs.at[j, k], xr.at[j, k], (c, xpeer),
+        )
+
+    def zcopy(j, k):
+        at = spans[j]
+        return remote(
+            zsend.at[k - 1, :, at], zbuf.at[k - 1, :, at],
+            zs.at[j, k - 1], zr.at[j, k - 1], (c, (z + k) % 4 * 2 + x),
+        )
+
+    def start(j):
+        for k in (2, 1, 3, 0):
+            xcopy(j, k).start()
+
+    def forward(j):
+        at = spans[j]
+        for k in (2, 1, 3):
+            xcopy(j, k).wait_recv()
+            own = part[block_of((z + k) % 4 * 2 + x, rows), at].astype(F32)
+            zsend[k - 1, :, at] = (own + xbuf[k, :, at].astype(F32)).astype(BF16)
+            zcopy(j, k).start()
+
+    def finish(j):
+        at = spans[j]
+        xcopy(j, 0).wait_recv()
+        total = part[block_of(e, rows), at].astype(F32) + xbuf[0, :, at].astype(F32)
+        for k in (1, 3, 2):
+            zcopy(j, k).wait_recv()
+            total += zbuf[k - 1, :, at].astype(F32)
+        return total
+
+    def drain():
+        for j in range(len(spans)):
+            for k in range(4):
+                xcopy(j, k).wait_send()
+            for k in (1, 2, 3):
+                zcopy(j, k).wait_send()
+
+    return start, forward, finish, drain
+
+
+def middle_kernel(
+    part_ref, stat_ref, wout_hbm, residual_ref, gain_ref,
+    attn_ref, routed_ref, squares_ref,
+    wout, gotp, gots, mixed, ysendp, ysends, ygotp, ygots, heads_out, product,
+    xbuf, zsend, zbuf, rows_all, sq_all,
+    wsem, s1, r1, s2, r2, s3, r3, xs, xr, zs, zr, gs, gr, fs, fr,
+):
+    c, e, core, z, x, sibling, across, xpeer = places()
+    load = pltpu.make_async_copy(wout_hbm, wout, wsem)
+    load.start()
+    greet()
+    half = gotp.shape[0]
+    heads = gotp.shape[1] // 128
+    pieces = 4
+    width = gotp.shape[1] // pieces
+    mine, theirs = block_of(core, half), block_of(1 - core, half)
+    first = [
+        remote(stat_ref.at[theirs, :], gots, s1.at[0], r1.at[0], (sibling, e)),
+        remote(part_ref.at[theirs, :], gotp, s1.at[1], r1.at[1], (sibling, e)),
+    ]
+    for copy in first:
+        copy.start()
+
+    def join(own_stat, other_stat):
+        lane = lax.broadcasted_iota(jnp.int32, own_stat.shape, 1)
+        is_top = lane < heads
+        top = jnp.maximum(own_stat, other_stat)
+        own_factor = jnp.exp2(jnp.where(is_top, own_stat - top, 0.0))
+        other_factor = jnp.exp2(jnp.where(is_top, other_stat - top, 0.0))
+        own_wide = pltpu.roll(own_factor, heads, 1)
+        other_wide = pltpu.roll(other_factor, heads, 1)
+        total = own_stat * own_wide + other_stat * other_wide
+        return jnp.where(is_top, top, total), own_factor, other_factor
+
+    first[0].wait_recv()
+    stat, own_factor, other_factor = join(stat_ref[mine, :], gots[...])
+    ysends[...] = stat
+    second_stat = remote(ysends, ygots, s2.at[pieces], r2.at[pieces], (across, e))
+    second_stat.start()
+    first[1].wait_recv()
+    second, third = [], []
+    for j in range(pieces):
+        for h in range(j * heads // pieces, (j + 1) * heads // pieces):
+            at = slice(h * 128, (h + 1) * 128)
+            value = part_ref[mine, at].astype(F32) * own_factor[:, h : h + 1]
+            value += gotp[:, at].astype(F32) * other_factor[:, h : h + 1]
+            mixed[:, at] = value
+            ysendp[:, at] = value.astype(BF16)
+        at = pl.ds(j * width, width)
+        second.append(remote(ysendp.at[:, at], ygotp.at[:, at], s2.at[j], r2.at[j], (across, e)))
+        second[j].start()
+    second_stat.wait_recv()
+    last, own_factor, other_factor = join(stat, ygots[...])
+    for j in range(pieces):
+        second[j].wait_recv()
+        for h in range(j * heads // pieces, (j + 1) * heads // pieces):
+            at = slice(h * 128, (h + 1) * 128)
+            value = mixed[:, at] * own_factor[:, h : h + 1]
+            value += ygotp[:, at].astype(F32) * other_factor[:, h : h + 1]
+            heads_out[mine, at] = (value / last[:, heads + h : heads + h + 1]).astype(BF16)
+        at = pl.ds(j * width, width)
+        third.append(
+            remote(heads_out.at[mine, at], heads_out.at[mine, at], s3.at[j], r3.at[j], (sibling, e))
+        )
+        third[j].start()
+    load.wait()
+    for copy in third:
+        copy.wait_recv()
+
+    columns = product.shape[1]
+    span = columns // 2
+    spans = [pl.ds(0, span), pl.ds(span, span)]
+    start, forward, finish, drain = scatter_sums(
+        product, xbuf, zsend, zbuf, xs, xr, zs, zr, spans
+    )
+    for j in range(2):
+        product[:, spans[j]] = jnp.dot(
+            heads_out[...], wout[:, spans[j]], preferred_element_type=F32
+        ).astype(BF16)
+        start(j)
+    forward(0)
+    forward(1)
+    rows = attn_ref.shape[0]
+    here = block_of(e, rows)
+    squares = jnp.zeros((rows, 1), F32)
+    for j in range(2):
+        at = spans[j]
+        total = finish(j)
+        attn_ref[:, at] = total.astype(BF16)
+        state = residual_ref[:, at].astype(F32) + total
+        rows_all[here, at] = (state * gain_ref[:, at].astype(F32)).astype(BF16)
+        squares += jnp.sum(state * state, axis=1, keepdims=True)
+    sq_all[here, :] = jnp.broadcast_to(squares, (rows, 128))
+
+    def zcopies(k):
+        to = (c, (z + k) % 4 * 2 + x)
+        return [
+            remote(a.at[here, :], a.at[here, :], gs.at[i, k], gr.at[i, k], to)
+            for i, a in enumerate((rows_all, sq_all))
+        ]
+
+    def xcopies(k):
+        block = block_of((z + 4 - k) % 4 * 2 + x, rows)
+        return [
+            remote(a.at[block, :], a.at[block, :], fs.at[i, k], fr.at[i, k], (c, xpeer))
+            for i, a in enumerate((rows_all, sq_all))
+        ]
+
+    for k in (2, 1, 3):
+        for copy in zcopies(k):
+            copy.start()
+    for copy in xcopies(0):
+        copy.start()
+    for k in (1, 3, 2):
+        for copy in zcopies(k):
+            copy.wait_recv()
+        for copy in xcopies(k):
+            copy.start()
+    for k in range(4):
+        for copy in xcopies(k):
+            copy.wait_recv()
+    for k in range(4):
+        for copy in xcopies(k):
+            copy.wait_send()
+    for k in (1, 2, 3):
+        for copy in zcopies(k):
+            copy.wait_send()
+    drain()
+    for copy in first + second + third + [second_stat]:
+        copy.wait_send()
+    routed_ref[...] = rows_all[...]
+    squares_ref[...] = sq_all[...]
+
+
+def middle(part, stat, w_out, residual, gain):
+    nodes, flat = part.shape
+    rows, columns = residual.shape
+    half = nodes // 2
+    vmem = pl.BlockSpec(memory_space=pltpu.VMEM)
+    dma = pltpu.SemaphoreType.DMA
+    return pl.pallas_call(
+        middle_kernel,
+        out_shape=(
+            jax.ShapeDtypeStruct((rows, columns), BF16),
+            jax.ShapeDtypeStruct((nodes, columns), BF16),
+            jax.ShapeDtypeStruct((nodes, 128), F32),
+        ),
+        in_specs=[vmem, vmem, pl.BlockSpec(memory_space=pl.ANY), vmem, vmem],
+        out_specs=(vmem, vmem, vmem),
+        scratch_shapes=[
+            pltpu.VMEM(w_out.shape, BF16),
+            pltpu.VMEM((half, flat), BF16),
+            pltpu.VMEM((half, 128), F32),
+            pltpu.VMEM((half, flat), F32),
+            pltpu.VMEM((half, flat), BF16),
+            pltpu.VMEM((half, 128), F32),
+            pltpu.VMEM((half, flat), BF16),
+            pltpu.VMEM((half, 128), F32),
+            pltpu.VMEM((nodes, flat), BF16),
+            pltpu.VMEM((nodes, columns), BF16),
+            pltpu.VMEM((4, rows, columns), BF16),
+            pltpu.VMEM((3, rows, columns), BF16),
+            pltpu.VMEM((3, rows, columns), BF16),
+            pltpu.VMEM((nodes, columns), BF16),
+            pltpu.VMEM((nodes, 128), F32),
+            dma, dma((2,)), dma((2,)), dma((5,)), dma((5,)), dma((4,)), dma((4,)),
+            dma((2, 4)), dma((2, 4)), dma((2, 3)), dma((2, 3)),
+            dma((2, 4)), dma((2, 4)), dma((2, 4)), dma((2, 4)),
+        ],
+        compiler_params=pltpu.CompilerParams(
+            collective_id=1, has_side_effects=True, vmem_limit_bytes=48 * MIB
+        ),
+        name="middle",
+    )(part, stat, w_out, residual, gain)
+
+
+def expert_kernel(
+    routed_ref, squares_ref, placing_ref, weighting_ref, wg_hbm, wu_hbm, wd_hbm,
+    moe_ref,
+    wgu, wd, chosen, own, send1, got1, send2, got2, hidden, moe, product,
+    xbuf, zsend, zbuf, sq_send, sq_got,
+    gusem, dsem, s1, r1, s2, r2, s3, r3, qs, qr, xs, xr, zs, zr,
+):
+    c, e, core, z, x, sibling, across, xpeer = places()
+    experts, slots, nodes = placing_ref.shape
+    ff = wg_hbm.shape[2]
+    half = slots // 2
+    mine, theirs = block_of(core, half), block_of(1 - core, half)
+    nt = (((1,), (1,)), ((), ()))
+
+    def load_gu(j, slot, i):
+        source = (wg_hbm, wu_hbm)[i]
+        return pltpu.make_async_copy(source.at[j], wgu.at[slot, i], gusem.at[slot, i])
+
+    def load_d(j):
+        return pltpu.make_async_copy(wd_hbm.at[j], wd.at[j], dsem.at[j])
+
+    for j in (0, 1):
+        for i in (0, 1):
+            load_gu(j, j, i).start()
+    greet()
+    sq_send[...] = jnp.transpose(squares_ref[...])[:8, :]
+
+    def sq_copy(i):
+        to = (sibling, across)[i]
+        return remote(sq_send, sq_got.at[i], qs.at[i], qr.at[i], (to, e))
+
+    sq_copy(0).start()
+
+    def copy1(j):
+        return remote(send1.at[j], got1.at[j], s1.at[j], r1.at[j], (sibling, e))
+
+    def copy2(j):
+        return remote(send2.at[j], got2.at[j], s2.at[j], r2.at[j], (across, e))
+
+    def copy3(j):
+        there = hidden.at[j, mine, :]
+        return remote(there, there, s3.at[j], r3.at[j], (sibling, e))
+
+    def ins(j, carry):
+        slot = j % 2
+        chosen[...] = jnp.dot(
+            placing_ref[j], routed_ref[...], preferred_element_type=F32
+        ).astype(BF16)
+        for i in range(2):
+            load_gu(j, slot, i).wait()
+            own[:, i * ff : (i + 1) * ff] = jnp.dot(
+                chosen[...], wgu[slot, i], preferred_element_type=F32
+            )
+        send1[j] = own[theirs, :].astype(BF16)
+        copy1(j).start()
+
+        @pl.when(j + 2 < experts)
+        def _():
+            for i in (0, 1):
+                load_gu(j + 2, slot, i).start()
+
+        @pl.when(j + 2 >= experts)
+        def _():
+            for d in range(2):
+                load_d((j + 2 - experts) * 2 + d).start()
+
+        copy1(j).wait_recv()
+        summed = own[mine, :] + got1[j].astype(F32)
+        send2[j] = summed.astype(BF16)
+        copy2(j).start()
+        return carry
+
+    lax.fori_loop(0, experts, ins, 0)
+    sq_copy(0).wait_recv()
+    sq_copy(0).wait_send()
+    sq_send[...] += sq_got[0]
+    sq_copy(1).start()
+    sq_copy(1).wait_recv()
+    square_sum = sq_send[...] + sq_got[1]
+    square_high = square_sum.astype(BF16)
+    square_low = (square_sum - square_high.astype(F32)).astype(BF16)
+
+    def middle_step(j, carry):
+        place = placing_ref[j, mine, :]
+        square = lax.dot_general(place, square_high, nt, preferred_element_type=F32)
+        square += lax.dot_general(place, square_low, nt, preferred_element_type=F32)
+        root = jnp.sqrt(square[:, :1] / D + 1e-06)
+        copy2(j).wait_recv()
+        total = send2[j].astype(F32) + got2[j].astype(F32)
+        gate, up = total[:, :ff] / root, total[:, ff:] / root
+        hidden[j, mine, :] = (gate / (1.0 + jnp.exp(-gate)) * up).astype(BF16)
+        copy3(j).start()
+        return carry
+
+    columns = moe.shape[1]
+    span = columns // 2
+    spans = [pl.ds(0, span), pl.ds(span, span)]
+
+    def out_step(j, carry):
+        copy3(j).wait_recv()
+        load_d(j).wait()
+        for at in spans:
+            answer = jnp.dot(hidden[j], wd[j, :, at], preferred_element_type=F32).astype(BF16)
+            add = jnp.dot(weighting_ref[j], answer, preferred_element_type=F32)
+            moe[:, at] += add
+        return carry
+
+    moe[...] = jnp.zeros_like(moe)
+    middle_step(0, 0)
+
+    def both(j, carry):
+        out_step(j - 1, 0)
+        return middle_step(j, carry)
+
+    lax.fori_loop(1, experts, both, 0)
+    start, forward, finish, drain = scatter_sums(
+        product, xbuf, zsend, zbuf, xs, xr, zs, zr, spans
+    )
+    final = experts - 1
+    copy3(final).wait_recv()
+    load_d(final).wait()
+    for i, at in enumerate(spans):
+        answer = jnp.dot(hidden[final], wd[final, :, at], preferred_element_type=F32).astype(BF16)
+        add = jnp.dot(weighting_ref[final], answer, preferred_element_type=F32)
+        product[:, at] = (moe[:, at] + add).astype(BF16)
+        start(i)
+    forward(0)
+    forward(1)
+    for j in range(2):
+        moe_ref[:, spans[j]] = finish(j).astype(BF16)
+    drain()
+    sq_copy(1).wait_send()
+
+    def settle(j, carry):
+        copy1(j).wait_send()
+        copy2(j).wait_send()
+        copy3(j).wait_send()
+        return carry
+
+    lax.fori_loop(0, experts, settle, 0)
+
+
+def run_experts(routed, squares, placing, weighting, w_gate, w_up, w_down, rows):
+    nodes, columns = routed.shape
+    experts, slots, _ = placing.shape
+    ff = w_gate.shape[2]
+    half = slots // 2
+    vmem = pl.BlockSpec(memory_space=pltpu.VMEM)
+    hbm = pl.BlockSpec(memory_space=pl.ANY)
+    dma = pltpu.SemaphoreType.DMA
+    return pl.pallas_call(
+        expert_kernel,
+        out_shape=jax.ShapeDtypeStruct((rows, columns), BF16),
+        in_specs=[vmem] * 4 + [hbm] * 3,
+        out_specs=vmem,
+        scratch_shapes=[
+            pltpu.VMEM((2, 2, columns, ff), BF16),
+            pltpu.VMEM((experts, ff, columns), BF16),
+            pltpu.VMEM((slots, columns), BF16),
+            pltpu.VMEM((slots, 2 * ff), F32),
+            pltpu.VMEM((experts, half, 2 * ff), BF16),
+            pltpu.VMEM((experts, half, 2 * ff), BF16),
+            pltpu.VMEM((experts, half, 2 * ff), BF16),
+            pltpu.VMEM((experts, half, 2 * ff), BF16),
+            pltpu.VMEM((experts, slots, ff), BF16),
+            pltpu.VMEM((nodes, columns), F32),
+            pltpu.VMEM((nodes, columns), BF16),
+            pltpu.VMEM((4, rows, columns), BF16),
+            pltpu.VMEM((3, rows, columns), BF16),
+            pltpu.VMEM((3, rows, columns), BF16),
+            pltpu.VMEM((8, nodes), F32),
+            pltpu.VMEM((2, 8, nodes), F32),
+            dma((2, 2)), dma((experts,)),
+            dma((experts,)), dma((experts,)), dma((experts,)), dma((experts,)),
+            dma((experts,)), dma((experts,)), dma((2,)), dma((2,)),
+            dma((2, 4)), dma((2, 4)), dma((2, 3)), dma((2, 3)),
+        ],
+        compiler_params=pltpu.CompilerParams(
+            collective_id=2, has_side_effects=True, vmem_limit_bytes=52 * MIB
+        ),
+        name="experts",
+    )(routed, squares, placing, weighting, w_gate, w_up, w_down)
+
+
+def slot_tables(routes, route_weights, rows, first, experts_here):
+    nodes = routes.shape[0]
+    capacity = max(2, 2 * rows * TOPK // EXPERTS)
+    slots = nodes // rows * capacity
+    hot = routes[:, :, None] == first + jnp.arange(experts_here, dtype=jnp.int32)
+    taken = jnp.any(hot, axis=1)
+    weight = jnp.sum(jnp.where(hot, route_weights[:, :, None], 0.0), axis=1)
+    node = jnp.arange(nodes, dtype=jnp.int32)
+    earlier = (node[None, :] < node[:, None]) & (node[None, :] // rows == node[:, None] // rows)
+    rank = jnp.dot(
+        earlier.astype(BF16), taken.astype(BF16), preferred_element_type=F32
+    ).astype(jnp.int32)
+    place = jnp.where(taken, (node // rows * capacity)[:, None] + rank, -1).T
+    slot = jnp.arange(slots, dtype=jnp.int32)
+    placing = (place[:, None, :] == slot[None, :, None]).astype(BF16)
+    weighting = jnp.where(
+        place[:, :, None] == slot[None, None, :], weight.T[:, :, None], 0.0
+    ).astype(BF16)
+    return placing, weighting
+
+
+def kernel_body(
+    prompt_cache, tree_latent, parents, query_nope, query_rope, w_absorb, w_value, w_out,
+    residual, norm_gain, routes, route_weights, w_gate, w_up, w_down,
+):
+    nodes = query_nope.shape[0]
+    rows = residual.shape[0]
+    node = jnp.arange(nodes, dtype=jnp.int32)
+    linked = ((parents[:, None] == node[None, :]) | (node[:, None] == node[None, :])).astype(BF16)
+    tree_rows = tree_latent.shape[0]
+    own_keys = lax.axis_index("ctx") * tree_rows + jnp.arange(tree_rows, dtype=jnp.int32)
+    select = (node[:, None] == own_keys[None, :]).astype(BF16)
+    experts_here = w_gate.shape[0]
+    placing, weighting = slot_tables(
+        routes, route_weights, rows, lax.axis_index("exp") * experts_here, experts_here
+    )
+    part, stat = attention(
+        query_nope.reshape(nodes, -1), query_rope.transpose(1, 0, 2),
+        w_absorb, w_value, prompt_cache, tree_latent, linked, select,
+    )
+    attn_out, routed, squares = middle(part, stat, w_out, residual, norm_gain.reshape(1, -1))
+    moe_out = run_experts(
+        routed, squares, placing, weighting, w_gate, w_up, w_down, rows
+    )
+    return attn_out, moe_out
+
+
 def solution(mesh):
+    body = kernel_body if (mesh.shape["ctx"], mesh.shape["exp"]) == (4, 8) else plain_body
     placed = (
         P("ctx", None),
         P("ctx", None),

time: 452 us -> 181 us (0.40); the launches traced: 447 us -> 181 us
  Pallas kernels: 0 us -> 167 us
  waiting for transfers between devices: 162 us -> 0 us
  matrix products: 116 us -> 0.24 us
  blocking collectives: 73.2 us -> 0 us
  other arithmetic: 38.4 us -> 0.73 us
  local copies, waits for them, and re-layouts: 36.8 us -> 12.1 us
  between operations: 14.3 us -> 0.81 us
  starting transfers between devices: 5.63 us -> 0 us
    pallas_call x0 -> x3, Pallas kernels: none -> 167 us  [the longest x1 59.6 us: run_experts(): pl.pallas_call(expert_kernel, out_shape=jax.ShapeDtypeStruct((rows, colum...]
    dot_general x23 -> x1, matrix products: 116 us -> 0.24 us  [slot_tables(): jnp.dot(earlier.astype(BF16), taken.astype(BF16), preferred_element_type=...]
    reduce_scatter x1 -> x0, waiting for transfers between devices: 61.2 us -> none  [body(): lax.psum_scatter(jnp.dot(heads_out, w_out, preferred_element_type=jnp.flo...]
    all_to_all x2 -> x0, blocking collectives: 54.1 us -> none  [the longest x1 44.2 us: body(): lax.all_to_all(send_blocks, 'exp', split_axis=0, concat_axis=0, tiled=True)]
    all_to_all x1 -> x0, waiting for transfers between devices: 41.7 us -> none  [body(): lax.all_to_all(answers, 'exp', split_axis=0, concat_axis=0, tiled=True)]
    psum x1 -> x0, waiting for transfers between devices: 33.7 us -> none  [expert_block(): lax.psum(up_part.astype(jnp.bfloat16), 'ctx').astype(jnp.float32)]
    convert_element_type x4 -> x0, local copies, waits for them, and re-layouts: 29.7 us -> none  [the longest x1 27.1 us: body(): prompt_exp.reshape(node_total * heads_here, -1).astype(jnp.bfloat16)]
    convert_element_type x10 -> x4, other arithmetic: 28.1 us -> 0.54 us  [the longest x1 0.34 us: slot_tables(): weighting = jnp.where(place[:, :, None] == slot[None, None, :], weight.T[...]
  transfers between devices with their start and end apart: 4 -> 0, of which waited for: 4 -> 0; matrix products, arithmetic and copies ran while one was open for 1% -> 0% of each run, Pallas kernels for 0% -> 0%
where the time goes in v1:
time: 181 us
  Pallas kernels  167 us (92%)
  local copies, waits for them, and re-layouts  12.1 us (7%)
    pallas_call x1, Pallas kernels, run_experts(): pl.pallas_call(expert_kernel, out_shape=jax.ShapeDtypeStruct((rows, colum...  59.6 us
    pallas_call x1, Pallas kernels, middle(): pl.pallas_call(middle_kernel, out_shape=(jax.ShapeDtypeStruct((rows, colu...  55.9 us
    pallas_call x1, Pallas kernels, attention(): pl.pallas_call(kernel, grid=(heads // per,), out_shape=(jax.ShapeDtypeStr...  51.4 us
    unnamed x19, local copies, waits for them, and re-layouts  12.1 us

profile of v1, /device:TPU:0, one launch (start us, length us, event | category | flops | bytes accessed | tf_op | source)
XLA Modules:
  0.0 180.8 jit_solution(16799973929127563761)
XLA Ops:
  0.6 0.0 copy-start.2
  0.6 0.0 copy-start.6
  0.7 1.5 copy.25
  2.2 1.5 copy.21
  3.7 0.0 copy-start.5
  3.7 0.0 copy-start.1
  3.7 6.1 %copy.22.refs_4_ = bf16[3072,576]{1,0:T(8,128)(2,1)} copy(bf16[3072,576]{0,1:T(8,128)(2,1)} %param.15) | data formatting | bytes 7077888 | tf_op args[0]
  9.9 0.0 copy-done.6
  9.9 0.1 fusion.4.refs_6_
  10.0 0.0 copy-done.2
  10.0 0.0 copy-start
  10.1 1.6 copy-done
  11.6 0.0 copy-start.3
  11.6 0.0 copy-start.4
  11.6 51.4 %attention.1 = (bf16[256,2048]{1,0:T(8,128)(2,1)S(1)}, f32[256,128]{1,0:T(8,128)S(1)}) custom-call(bf16[256,2048]{1,0:T(8,128)(2,1)S(1)} %bitcast.9, bf16[16,256,64]{2,1,0:T(8,128)(2,1)S(1)} %bitcast.10, bf16[16,128,512]{2,1,0:T(8,128)(2,1)S(1)} %copy-done, bf16[16,512,128]{2,1,0:T(8,128)(2,1)} %refs_3_.1, bf16[3072,576]{1,0:T(8,128)(2,1)} %copy.22.refs_4_, ...), custom_call_target="tpu_custom_call" | custom-call | tf_op jit(solution)/shard_map/attention/pallas_call | solution.py:290
  63.1 0.0 copy-done.5
  63.1 0.0 copy-done.1
  63.1 55.9 %middle.1 = (bf16[32,1792]{1,0:T(8,128)(2,1)S(1)}, bf16[256,1792]{1,0:T(8,128)(2,1)S(1)}, f32[256,128]{1,0:T(8,128)S(1)}) custom-call(bf16[256,2048]{1,0:T(8,128)(2,1)S(1)} %get-tuple-element.7.part_ref, f32[256,128]{1,0:T(8,128)S(1)} %get-tuple-element.8.stat_ref, bf16[2048,1792]{1,0:T(8,128)(2,1)} %wout_hbm.1, bf16[32,1792]{1,0:T(8,128)(2,1)S(1)} %copy-done.1, ...), custom_call_target="tpu_custom_call" | custom-call | tf_op jit(solution)/shard_map/middle/pallas_call | solution.py:532
  119.1 0.0 copy-done.3
  119.1 0.1 compare_reduce_fusion
  119.2 0.2 fusion.1
  119.4 0.1 fusion.2.placing_ref
  119.5 0.0 copy-done.4
  119.5 0.1 fusion.11
  119.6 0.3 select_convert_fusion.weighting_ref
  120.0 59.6 %experts.1 = bf16[32,1792]{1,0:T(8,128)(2,1)S(1)} custom-call(bf16[256,1792]{1,0:T(8,128)(2,1)S(1)} %get-tuple-element.10.routed_ref, f32[256,128]{1,0:T(8,128)S(1)} %get-tuple-element.11.squares_ref, bf16[4,128,256]{2,1,0:T(8,128)(2,1)S(1)} %fusion.2.placing_ref, bf16[4,256,128]{2,1,0:T(8,128)(2,1)S(1)} %select_convert_fusion.weighting_ref, ...), custom_call_target="tpu_custom_call" | custom-call | tf_op jit(solution)/shard_map/experts/pallas_call | solution.py:718
  179.5 0.6 copy.28
  180.2 0.6 copy.29
  (5 shorter events, 0.0 us)
Async XLA Ops:
  0.6 9.4 %copy-start.2 = (bf16[64,576]{1,0:T(8,128)(2,1)S(1)}, bf16[64,576]{1,0:T(8,128)(2,1)}, u32[]{:S(2)}) copy-start(bf16[64,576]{1,0:T(8,128)(2,1)} %refs_5_.1) | copy-start | bytes 221188
  0.6 9.2 %copy-start.6 = (s32[256]{0:T(256)S(1)}, s32[256]{0:T(256)}, u32[]{:S(2)}) copy-start(s32[256]{0:T(256)} %param.17) | copy-start | bytes 3076
  3.7 59.4 %copy-start.5 = (bf16[1792]{0:T(1024)(128)(2,1)S(1)}, bf16[1792]{0:T(1024)(128)(2,1)}, u32[]{:S(2)}) copy-start(bf16[1792]{0:T(1024)(128)(2,1)} %param.24) | copy-start | bytes 10756
  3.7 59.4 %copy-start.1 = (bf16[32,1792]{1,0:T(8,128)(2,1)S(1)}, bf16[32,1792]{1,0:T(8,128)(2,1)}, u32[]{:S(2)}) copy-start(bf16[32,1792]{1,0:T(8,128)(2,1)} %residual_ref.1) | copy-start | bytes 344068
  10.0 1.6 copy-start
  11.6 107.4 %copy-start.3 = (s32[256,8]{0,1:T(8,128)S(1)}, s32[256,8]{0,1:T(8,128)}, u32[]{:S(2)}) copy-start(s32[256,8]{0,1:T(8,128)} %param.25) | copy-start | bytes 24580
  11.6 107.9 %copy-start.4 = (f32[256,8]{0,1:T(8,128)S(1)}, f32[256,8]{0,1:T(8,128)}, u32[]{:S(2)}) copy-start(f32[256,8]{0,1:T(8,128)} %param.26) | copy-start | bytes 24580

commit v2 on v1

--- a/solution.py
+++ b/solution.py
@@ -225,7 +225,7 @@
                         qn_ref[:, h * nope : (h + 1) * nope], wabs_ref[h],
                         preferred_element_type=F32,
                     ).astype(BF16),
-                    qr_ref[h],
+                    jnp.transpose(qr_ref[h].astype(F32)).astype(BF16),
                 ],
                 axis=1,
             )
@@ -233,12 +233,10 @@
         ],
         axis=0,
     )
-    keys = cache_ref.shape[0]
+    keys = cache_ref.shape[1]
     chunk = 512
     scores = [
-        lax.dot_general(
-            queries, cache_ref[at : at + chunk, :], nt, preferred_element_type=F32
-        ) * factor
+        jnp.dot(queries, cache_ref[:, at : at + chunk], preferred_element_type=F32) * factor
         for at in range(0, keys, chunk)
     ]
     tree_scores = lax.dot_general(queries, tree_ref[...], nt, preferred_element_type=F32) * factor
@@ -257,8 +255,8 @@
     for i, piece in enumerate(scores):
         weight = jnp.exp2(piece - top)
         sums = weight if sums is None else sums + weight
-        mix += jnp.dot(
-            weight.astype(BF16), cache_ref[i * chunk : (i + 1) * chunk, :latent],
+        mix += lax.dot_general(
+            weight.astype(BF16), cache_ref[:latent, i * chunk : (i + 1) * chunk], nt,
             preferred_element_type=F32,
         )
     total += jnp.sum(sums, axis=1, keepdims=True)
@@ -279,7 +277,7 @@
     nodes = qn.shape[0]
     heads, nope, latent = wabs.shape
     vdim = wval.shape[2]
-    rope = qr.shape[2]
+    rope = qr.shape[1]
     per = HEADS_PER_STEP
     whole = lambda a: pl.BlockSpec(a.shape, lambda i: (0,) * a.ndim)
     scale = float((nope + rope) ** (-0.5))
@@ -296,7 +294,7 @@
         ),
         in_specs=[
             pl.BlockSpec((nodes, per * nope), lambda i: (0, i)),
-            pl.BlockSpec((per, nodes, rope), lambda i: (i, 0, 0)),
+            pl.BlockSpec((per, rope, nodes), lambda i: (i, 0, 0)),
             pl.BlockSpec((per, nope, latent), lambda i: (i, 0, 0)),
             pl.BlockSpec((per, latent, vdim), lambda i: (i, 0, 0)),
             whole(cache), whole(tree), whole(linked), whole(select),
@@ -598,50 +596,64 @@
 
     sq_copy(0).start()
 
-    def copy1(j):
-        return remote(send1.at[j], got1.at[j], s1.at[j], r1.at[j], (sibling, e))
-
-    def copy2(j):
-        return remote(send2.at[j], got2.at[j], s2.at[j], r2.at[j], (across, e))
+    def copy1(j, i):
+        at = pl.ds(i * ff, ff)
+        return remote(
+            send1.at[j, :, at], got1.at[j, :, at], s1.at[j, i], r1.at[j, i], (sibling, e)
+        )
+
+    def copy2(j, i):
+        at = pl.ds(i * ff, ff)
+        return remote(
+            send2.at[j, :, at], got2.at[j, :, at], s2.at[j, i], r2.at[j, i], (across, e)
+        )
 
     def copy3(j):
         there = hidden.at[j, mine, :]
         return remote(there, there, s3.at[j], r3.at[j], (sibling, e))
+
+    def merge(j, i):
+        at = pl.ds(i * ff, ff)
+        copy1(j, i).wait_recv()
+        send2[j, :, at] = (own[i, mine, :] + got1[j, :, at].astype(F32)).astype(BF16)
+        copy2(j, i).start()
+
+    sq_copy(0).wait_recv()
+    sq_copy(0).wait_send()
+    sq_send[...] += sq_got[0]
+    sq_copy(1).start()
 
     def ins(j, carry):
         slot = j % 2
         chosen[...] = jnp.dot(
             placing_ref[j], routed_ref[...], preferred_element_type=F32
         ).astype(BF16)
-        for i in range(2):
+        for i in (0, 1):
             load_gu(j, slot, i).wait()
-            own[:, i * ff : (i + 1) * ff] = jnp.dot(
-                chosen[...], wgu[slot, i], preferred_element_type=F32
-            )
-        send1[j] = own[theirs, :].astype(BF16)
-        copy1(j).start()
-
-        @pl.when(j + 2 < experts)
-        def _():
-            for i in (0, 1):
+            own[i] = jnp.dot(chosen[...], wgu[slot, i], preferred_element_type=F32)
+            send1[j, :, pl.ds(i * ff, ff)] = own[i, theirs, :].astype(BF16)
+            copy1(j, i).start()
+
+            @pl.when(j + 2 < experts)
+            def _():
                 load_gu(j + 2, slot, i).start()
 
-        @pl.when(j + 2 >= experts)
-        def _():
-            for d in range(2):
-                load_d((j + 2 - experts) * 2 + d).start()
-
-        copy1(j).wait_recv()
-        summed = own[mine, :] + got1[j].astype(F32)
-        send2[j] = summed.astype(BF16)
-        copy2(j).start()
+            @pl.when(j + 2 >= experts)
+            def _():
+                load_d((j + 2 - experts) * 2 + i).start()
+
+            if i == 0:
+
+                @pl.when(j > 0)
+                def _():
+                    merge(j - 1, 1)
+
+            else:
+                merge(j, 0)
         return carry
 
     lax.fori_loop(0, experts, ins, 0)
-    sq_copy(0).wait_recv()
-    sq_copy(0).wait_send()
-    sq_send[...] += sq_got[0]
-    sq_copy(1).start()
+    merge(experts - 1, 1)
     sq_copy(1).wait_recv()
     square_sum = sq_send[...] + sq_got[1]
     square_high = square_sum.astype(BF16)
@@ -652,7 +664,8 @@
         square = lax.dot_general(place, square_high, nt, preferred_element_type=F32)
         square += lax.dot_general(place, square_low, nt, preferred_element_type=F32)
         root = jnp.sqrt(square[:, :1] / D + 1e-06)
-        copy2(j).wait_recv()
+        copy2(j, 0).wait_recv()
+        copy2(j, 1).wait_recv()
         total = send2[j].astype(F32) + got2[j].astype(F32)
         gate, up = total[:, :ff] / root, total[:, ff:] / root
         hidden[j, mine, :] = (gate / (1.0 + jnp.exp(-gate)) * up).astype(BF16)
@@ -699,8 +712,9 @@
     sq_copy(1).wait_send()
 
     def settle(j, carry):
-        copy1(j).wait_send()
-        copy2(j).wait_send()
+        for i in (0, 1):
+            copy1(j, i).wait_send()
+            copy2(j, i).wait_send()
         copy3(j).wait_send()
         return carry
 
@@ -724,7 +738,7 @@
             pltpu.VMEM((2, 2, columns, ff), BF16),
             pltpu.VMEM((experts, ff, columns), BF16),
             pltpu.VMEM((slots, columns), BF16),
-            pltpu.VMEM((slots, 2 * ff), F32),
+            pltpu.VMEM((2, slots, ff), F32),
             pltpu.VMEM((experts, half, 2 * ff), BF16),
             pltpu.VMEM((experts, half, 2 * ff), BF16),
             pltpu.VMEM((experts, half, 2 * ff), BF16),
@@ -738,7 +752,7 @@
             pltpu.VMEM((8, nodes), F32),
             pltpu.VMEM((2, 8, nodes), F32),
             dma((2, 2)), dma((experts,)),
-            dma((experts,)), dma((experts,)), dma((experts,)), dma((experts,)),
+            dma((experts, 2)), dma((experts, 2)), dma((experts, 2)), dma((experts, 2)),
             dma((experts,)), dma((experts,)), dma((2,)), dma((2,)),
             dma((2, 4)), dma((2, 4)), dma((2, 3)), dma((2, 3)),
         ],
@@ -786,8 +800,8 @@
         routes, route_weights, rows, lax.axis_index("exp") * experts_here, experts_here
     )
     part, stat = attention(
-        query_nope.reshape(nodes, -1), query_rope.transpose(1, 0, 2),
-        w_absorb, w_value, prompt_cache, tree_latent, linked, select,
+        query_nope.reshape(nodes, -1), query_rope.transpose(1, 2, 0),
+        w_absorb, w_value, prompt_cache.T, tree_latent, linked, select,
     )
     attn_out, routed, squares = middle(part, stat, w_out, residual, norm_gain.reshape(1, -1))
     moe_out = run_experts(

time: 181 us -> 169 us (0.934)
  Pallas kernels: 167 us -> 160 us
  local copies, waits for them, and re-layouts: 12.1 us -> 6.37 us
    pallas_call x1, Pallas kernels: 59.6 us -> 52.8 us  [run_experts(): pl.pallas_call(expert_kernel, out_shape=jax.ShapeDtypeStruct((rows, colum...]
    unnamed x19 -> x17, local copies, waits for them, and re-layouts: 12.1 us -> 6.36 us
where the time goes in v2:
time: 169 us
  Pallas kernels  160 us (95%)
  local copies, waits for them, and re-layouts  6.37 us (4%)
    pallas_call x1, Pallas kernels, middle(): pl.pallas_call(middle_kernel, out_shape=(jax.ShapeDtypeStruct((rows, colu...  55.9 us
    pallas_call x1, Pallas kernels, run_experts(): pl.pallas_call(expert_kernel, out_shape=jax.ShapeDtypeStruct((rows, colum...  52.8 us
    pallas_call x1, Pallas kernels, attention(): pl.pallas_call(kernel, grid=(heads // per,), out_shape=(jax.ShapeDtypeStr...  51.2 us
    unnamed x17, local copies, waits for them, and re-layouts  6.36 us

profile of v2, /device:TPU:0, one launch (start us, length us, event | category | flops | bytes accessed | tf_op | source)
XLA Modules:
  0.0 168.7 jit_solution(3939469043351621013)
XLA Ops:
  0.6 0.0 copy-start.2
  0.6 0.0 copy-start.6
  0.7 1.5 copy.21
  2.2 0.8 fusion.4.refs_6_
  3.0 0.0 copy-start
  3.0 1.6 copy-done
  4.6 0.0 copy-start.1
  4.6 1.0 copy-done.1
  5.7 0.0 copy-start.3
  5.7 0.9 copy-done.3
  6.5 0.0 copy-start.4
  6.6 0.0 copy-start.5
  6.6 51.2 %attention.1 = (bf16[256,2048]{1,0:T(8,128)(2,1)S(1)}, f32[256,128]{1,0:T(8,128)S(1)}) custom-call(bf16[256,2048]{1,0:T(8,128)(2,1)S(1)} %bitcast.10, bf16[16,64,256]{2,1,0:T(8,128)(2,1)S(1)} %bitcast.11, bf16[16,128,512]{2,1,0:T(8,128)(2,1)S(1)} %copy-done, bf16[16,512,128]{2,1,0:T(8,128)(2,1)} %refs_3_.1, bf16[576,3072]{1,0:T(8,128)(2,1)} %bitcast.12, ...), custom_call_target="tpu_custom_call" | custom-call | tf_op jit(solution)/shard_map/attention/pallas_call | solution.py:288
  57.7 0.0 copy-done.6
  57.8 0.0 copy-done.2
  57.8 55.9 %middle.1 = (bf16[32,1792]{1,0:T(8,128)(2,1)S(1)}, bf16[256,1792]{1,0:T(8,128)(2,1)S(1)}, f32[256,128]{1,0:T(8,128)S(1)}) custom-call(bf16[256,2048]{1,0:T(8,128)(2,1)S(1)} %get-tuple-element.7.part_ref, f32[256,128]{1,0:T(8,128)S(1)} %get-tuple-element.8.stat_ref, bf16[2048,1792]{1,0:T(8,128)(2,1)} %wout_hbm.1, bf16[32,1792]{1,0:T(8,128)(2,1)S(1)} %copy-done.2, ...), custom_call_target="tpu_custom_call" | custom-call | tf_op jit(solution)/shard_map/middle/pallas_call | solution.py:530
  113.7 0.0 copy-done.4
  113.7 0.1 compare_reduce_fusion
  113.8 0.2 fusion.1
  114.1 0.1 fusion.2.placing_ref
  114.2 0.0 copy-done.5
  114.2 0.1 fusion.11
  114.3 0.3 select_convert_fusion.weighting_ref
  114.6 52.8 %experts.1 = bf16[32,1792]{1,0:T(8,128)(2,1)S(1)} custom-call(bf16[256,1792]{1,0:T(8,128)(2,1)S(1)} %get-tuple-element.10.routed_ref, f32[256,128]{1,0:T(8,128)S(1)} %get-tuple-element.11.squares_ref, bf16[4,128,256]{2,1,0:T(8,128)(2,1)S(1)} %fusion.2.placing_ref, bf16[4,256,128]{2,1,0:T(8,128)(2,1)S(1)} %select_convert_fusion.weighting_ref, ...), custom_call_target="tpu_custom_call" | custom-call | tf_op jit(solution)/shard_map/experts/pallas_call | solution.py:732
  167.4 0.6 copy.24
  168.1 0.6 copy.25
  (5 shorter events, 0.0 us)
Async XLA Ops:
  0.6 57.1 %copy-start.2 = (bf16[32,1792]{1,0:T(8,128)(2,1)S(1)}, bf16[32,1792]{1,0:T(8,128)(2,1)}, u32[]{:S(2)}) copy-start(bf16[32,1792]{1,0:T(8,128)(2,1)} %residual_ref.1) | copy-start | bytes 344068
  0.6 57.1 %copy-start.6 = (bf16[1792]{0:T(1024)(128)(2,1)S(1)}, bf16[1792]{0:T(1024)(128)(2,1)}, u32[]{:S(2)}) copy-start(bf16[1792]{0:T(1024)(128)(2,1)} %param.24) | copy-start | bytes 10756
  3.0 1.6 copy-start
  4.6 1.0 copy-start.1
  5.7 0.9 copy-start.3
  6.5 107.2 %copy-start.4 = (s32[256,8]{0,1:T(8,128)S(1)}, s32[256,8]{0,1:T(8,128)}, u32[]{:S(2)}) copy-start(s32[256,8]{0,1:T(8,128)} %param.25) | copy-start | bytes 24580
  6.6 107.6 %copy-start.5 = (f32[256,8]{0,1:T(8,128)S(1)}, f32[256,8]{0,1:T(8,128)}, u32[]{:S(2)}) copy-start(f32[256,8]{0,1:T(8,128)} %param.26) | copy-start | bytes 24580
